TPU v7x, 128 devices: a whole 4x4x4 slice. The times are simulated.
128 devices in a mesh: front: 4 (over z_hi, core), tile: 32 (over z_lo, y, x).
Axes of the slice: x: 4, y: 4, z: 4 (z_hi: 2, z_lo: 2; z = z_hi * 2 + z_lo), core: 2. Of those that a mesh axis runs over, the one named last changes fastest.
Arguments:
- fronts: float32 [4, 32, 2048, 1024], P('front', 'tile')
- parents: bfloat16 [4, 32, 2048, 1024], P('front', 'tile'), may hold values from -3 to 3
- parent_of: int32 [4], replicated, may hold values from 0 to 3
- block_map: int32 [4, 48], replicated, may hold values from 0 to 63, as said below
Outputs:
- factor: bfloat16 [4, 32, 2048, 256], P('front', 'tile')
- merged: float32 [4, 32, 2048, 1024], P('front', 'tile')
Inputs may be any that keep to these rules, and one draw needn't show every extreme that they name: block_map[g, a] % 8 == a % 8, and the 48 entries of one front are distinct.
All inputs are finite; a program needn't handle non-finite values.
Results may differ from a plain program's by a relative error of at most 0.0032.
Values may be sent and summed in bfloat16 or wider, within the bound.
No kernel may reach another device: no remote copies, remote signals or barrier semaphores. Data moves between devices by JAX's collectives and lax.ppermute only.
A program may use at most 192 MiB of HBM per device.

v0:
```python
import jax
import jax.numpy as jnp
from jax import lax
from jax.sharding import PartitionSpec as P

BLK = 128
NPAN = 2
NP = 2048


def from_partner(value, axis, distance):
    return lax.ppermute(value, axis, [(i, i ^ 1 << distance) for i in range(lax.axis_size(axis))])


def per_device(fronts, parents, parent_of, block_map):
    tiles = lax.axis_size("tile")
    grid_rows = tiles // 8
    row_bits = grid_rows.bit_length() - 1
    tile_index = lax.axis_index("tile")
    grid_col = tile_index % 8
    grid_row = tile_index // 8
    row_offset = (grid_row + grid_rows - 1) % grid_rows
    tile_data = fronts[0, 0]
    tile_rows, tile_cols = tile_data.shape
    per_panel = 8 // grid_rows
    width = BLK * 8
    identity = jnp.eye(width, dtype=jnp.float32)
    factor_cols = []
    for panel_step in range(NPAN):
        row_start = panel_step * per_panel * BLK
        panel_piece = tile_data[row_start:, panel_step * BLK : (panel_step + 1) * BLK]
        corner = panel_piece[: per_panel * BLK]
        everyone = lax.all_gather(corner, "tile", axis=0, tiled=True)
        everyone = jnp.roll(everyone.reshape(grid_rows, 8, per_panel, BLK, BLK), -1, axis=0)
        diagonal = everyone.transpose(2, 0, 3, 1, 4).reshape(width, width)
        lower_factor = jnp.linalg.cholesky(diagonal)
        inverse = lax.linalg.triangular_solve(lower_factor, identity, left_side=True, lower=True)
        rows_now = panel_piece.shape[0]
        gathered = panel_piece
        for bit_no in range(3):
            my_bit = grid_col >> bit_no & 1
            received = from_partner(gathered, "tile", bit_no)
            gathered = jnp.where(
                my_bit == 0,
                jnp.concatenate([gathered, received], 1),
                jnp.concatenate([received, gathered], 1),
            )
        panel_vals = jnp.dot(
            gathered, inverse.T, precision=lax.Precision.HIGHEST, preferred_element_type=jnp.float32
        ).astype(jnp.bfloat16)
        share = lax.dynamic_slice_in_dim(panel_vals, grid_col * BLK, BLK, 1)
        factor_cols.append(jnp.concatenate([jnp.zeros((row_start, BLK), jnp.bfloat16), share], 0))
        groups = panel_vals.reshape(rows_now // (per_panel * BLK), per_panel, BLK, width)
        picked = lax.dynamic_index_in_dim(groups, grid_col // grid_rows, 1, keepdims=False)[1:]
        picked = picked.reshape(-1, width)
        source = (grid_col + 1) % grid_rows
        for bit_no in range(row_bits):
            has_data = (grid_row ^ source) >> bit_no == 0
            received = from_partner(picked, "tile", 3 + bit_no)
            picked = jnp.where(has_data, picked, received)
        trailing = panel_vals[per_panel * BLK :]
        update = lax.dot_general(
            trailing, picked, (((1,), (1,)), ((), ())), preferred_element_type=jnp.float32
        )
        tile_data = tile_data.at[row_start + per_panel * BLK :, (panel_step + 1) * BLK :].add(
            -update
        )
    factor_tile = jnp.concatenate(factor_cols, 1)
    contribution = tile_data[NP // grid_rows :, NP // 8 :].astype(jnp.bfloat16)[None]
    my_front = lax.axis_index("front")
    rows_blocks = contribution.shape[1] // BLK
    cols_blocks = contribution.shape[2] // BLK
    row_targets = jnp.arange(rows_blocks) * grid_rows + row_offset
    col_targets = jnp.arange(cols_blocks) * 8 + grid_col
    start_accum = (
        parents[0, 0].astype(jnp.float32).reshape(tile_rows // BLK, BLK, tile_cols // BLK, BLK)
    )
    accum = start_accum
    arrived = lax.all_gather(contribution, "front", axis=0, tiled=True)
    first_child = jnp.int32(0)
    for member in range(arrived.shape[0]):
        child_id = first_child + member
        mapping = lax.dynamic_index_in_dim(block_map, child_id, 0, keepdims=False)
        target_rows = jnp.take(mapping, row_targets) // grid_rows
        target_cols = jnp.take(mapping, col_targets) // 8
        owner = lax.dynamic_index_in_dim(parent_of, child_id, 0, keepdims=False)
        weight = (owner == my_front).astype(jnp.float32)
        blocks = (
            arrived[member]
            .astype(jnp.float32)
            .reshape(rows_blocks, BLK, cols_blocks, BLK)
            .transpose(0, 2, 1, 3)
        )
        accum = accum.at[target_rows[:, None], :, target_cols[None, :], :].add(weight * blocks)
    return (factor_tile[None, None], accum.reshape(tile_rows, tile_cols)[None, None])


def solution(mesh):
    return jax.shard_map(
        per_device,
        mesh=mesh,
        in_specs=(P("front", "tile", None, None), P("front", "tile", None, None), P(), P()),
        out_specs=(P("front", "tile", None, None), P("front", "tile", None, None)),
        check_vma=False,
    )
```

profile of v0, /device:TPU:16, one launch (start us, length us, event | category | flops | bytes accessed | tf_op | source)
XLA Modules:
  0.0 1546.7 jit_solution(17580803621772040282)
XLA Ops:
  11.7 32.3 %collective-permute-done = f32[2048,128]{1,0:T(8,128)} collective-permute-done((f32[2048,128]{1,0:T(8,128)S(1)}, f32[2048,128]{1,0:T(8,128)}, u32[]{:S(2)}, u32[]{:S(2)}) %collective-permute-start) | collective-permute-done | bytes 1048608 | tf_op jit(solution)/shard_map/ppermute | solution.py:12
  50.7 53.4 %collective-permute-done.1 = f32[2048,256]{1,0:T(8,128)} collective-permute-done((f32[2048,256]{1,0:T(8,128)S(1)}, f32[2048,256]{1,0:T(8,128)}, u32[]{:S(2)}, u32[]{:S(2)}) %collective-permute-start.1) | collective-permute-done | bytes 2097184 | tf_op jit(solution)/shard_map/ppermute | solution.py:12
  109.3 73.7 %all-gather.5.cloned.1.call-done = f32[8192,128]{1,0:T(8,128)} async-done(((f32[256,128]{1,0:T(8,128)}), f32[8192,128]{1,0:T(8,128)}) %all-gather.5.cloned.1.call-update) | async-done | bytes 4194320 | tf_op jit(solution)/shard_map/all_gather | solution.py:33
  215.9 11.7 cholesky.619
  243.9 12.1 cholesky.638
  269.8 11.7 cholesky.659
  295.4 11.9 cholesky.678
  321.2 11.7 cholesky.697
  346.8 11.7 cholesky.716
  372.1 11.7 cholesky.735
  397.0 11.7 cholesky.752
  424.0 23.3 %while.6 = (s32[]{:T(128)}, f32[1024,1024]{1,0:T(8,128)}, s32[8,2]{0,1:T(2,128)S(1)}, f32[8,128,128]{2,1,0:T(8,128)S(1)}, s32[]{:T(128)}) while((s32[]{:T(128)}, f32[1024,1024]{1,0:T(8,128)}, s32[8,2]{0,1:T(2,128)S(1)}, f32[8,128,128]{2,1,0:T(8,128)S(1)}, s32[]{:T(128)}) %tuple.150), condition=%wide.while_cond.2, body=%wide.while_body.2.sunk | while | flops 2 | bytes 131189 | solution.py:37
  447.3 78.8 %custom-call.70 = f32[8,128,128]{1,2,0:T(8,128)S(1)} custom-call(f32[8,128,128]{2,1,0:T(8,128)S(1)} %get-tuple-element.44), custom_call_target="InvertDiagBlocksLowerTriangular" | custom-call | tf_op jit(solution)/shard_map/triangular_solve/custom-call.7 | solution.py:37
  549.5 31.1 %fusion.17 = bf16[2048,1024]{1,0:T(8,128)(2,1)S(1)} fusion(f32[1024,1024]{1,0:T(8,128)S(1)} %convolution_dynamic-update-slice_fusion.1, f32[2048,512]{1,0:T(8,128)} %collective-permute-done.2, f32[2048,512]{1,0:T(8,128)} %maximum_select_fusion.4, pred[]{:T(512)S(6)} %eq.42), kind=kOutput, calls=%fused_computation.51 | convolution fusion | flops 25778192384 | bytes 16777216 | tf_op jit(solution)/shard_map/dot_general | solution.py:48
  590.2 26.1 %collective-permute-done.3 = bf16[896,1024]{1,0:T(8,128)(2,1)} collective-permute-done((bf16[896,1024]{1,0:T(8,128)(2,1)S(1)}, bf16[896,1024]{1,0:T(8,128)(2,1)}, u32[]{:S(2)}, u32[]{:S(2)}) %collective-permute-start.3) | collective-permute-done | bytes 1835040 | tf_op jit(solution)/shard_map/ppermute | solution.py:12
  659.2 30.2 %collective-permute-done.5 = f32[1792,128]{0,1:T(8,128)S(1)} collective-permute-done((f32[1792,128]{0,1:T(8,128)S(1)}, f32[1792,128]{0,1:T(8,128)S(1)}, u32[]{:S(2)}, u32[]{:S(2)}) %collective-permute-start.5) | collective-permute-done | bytes 917536 | tf_op jit(solution)/shard_map/ppermute | solution.py:12
  689.7 30.8 %collective-permute-done.6 = f32[1792,256]{0,1:T(8,128)} collective-permute-done((f32[1792,256]{0,1:T(8,128)S(1)}, f32[1792,256]{0,1:T(8,128)}, u32[]{:S(2)}, u32[]{:S(2)}) %collective-permute-start.6) | collective-permute-done | bytes 1835040 | tf_op jit(solution)/shard_map/ppermute | solution.py:12
  725.3 95.2 %all-gather.7.cloned.1.call-done = f32[8192,128]{0,1:T(8,128)} async-done(((f32[256,128]{0,1:T(8,128)}), f32[8192,128]{0,1:T(8,128)}) %all-gather.7.cloned.1.call-update) | async-done | bytes 4194320 | tf_op jit(solution)/shard_map/all_gather | solution.py:33
  855.6 11.7 cholesky.767
  883.6 11.9 cholesky.786
  935.0 12.1 cholesky.826
  1064.2 23.2 %while.7 = (s32[]{:T(128)}, f32[1024,1024]{1,0:T(8,128)}, s32[8,2]{0,1:T(2,128)S(1)}, f32[8,128,128]{2,1,0:T(8,128)S(1)}, s32[]{:T(128)}) while((s32[]{:T(128)}, f32[1024,1024]{1,0:T(8,128)}, s32[8,2]{0,1:T(2,128)S(1)}, f32[8,128,128]{2,1,0:T(8,128)S(1)}, s32[]{:T(128)}) %tuple.162), condition=%wide.while_cond.2.clone, body=%wide.while_body.2.clone.sunk | while | flops 2 | bytes 131189 | solution.py:37
  1087.5 79.0 %custom-call.78 = f32[8,128,128]{1,2,0:T(8,128)S(1)} custom-call(f32[8,128,128]{2,1,0:T(8,128)S(1)} %get-tuple-element.45), custom_call_target="InvertDiagBlocksLowerTriangular" | custom-call | tf_op jit(solution)/shard_map/triangular_solve/custom-call.7 | solution.py:37
  1189.9 50.8 %fusion.18 = bf16[1792,1024]{1,0:T(8,128)(2,1)S(1)} fusion(f32[1024,1024]{1,0:T(8,128)S(1)} %convolution_dynamic-update-slice_fusion, f32[1792,512]{0,1:T(8,128)} %collective-permute-done.7, f32[1792,512]{0,1:T(8,128)} %maximum_select_fusion.9, pred[]{:T(512)S(6)} %eq.42), kind=kOutput, calls=%fused_computation.52 | convolution fusion | flops 22555918336 | bytes 15204353 | tf_op jit(solution)/shard_map/dot_general | solution.py:48
  1250.8 18.4 %collective-permute-done.8 = bf16[768,1024]{1,0:T(8,128)(2,1)S(1)} collective-permute-done((bf16[768,1024]{1,0:T(8,128)(2,1)S(1)}, bf16[768,1024]{1,0:T(8,128)(2,1)S(1)}, u32[]{:S(2)}, u32[]{:S(2)}) %collective-permute-start.8) | collective-permute-done | bytes 1572896 | tf_op jit(solution)/shard_map/ppermute | solution.py:12
  1271.6 18.9 %collective-permute-done.9 = bf16[768,1024]{1,0:T(8,128)(2,1)S(1)} collective-permute-done((bf16[768,1024]{1,0:T(8,128)(2,1)S(1)}, bf16[768,1024]{1,0:T(8,128)(2,1)S(1)}, u32[]{:S(2)}, u32[]{:S(2)}) %collective-permute-start.9) | collective-permute-done | bytes 1572896 | tf_op jit(solution)/shard_map/ppermute | solution.py:12
  1318.3 47.8 %all-gather.9.cloned.1.call-done = bf16[6144,768]{0,1:T(8,128)(2,1)} async-done(((bf16[1536,768]{0,1:T(8,128)(2,1)}), bf16[6144,768]{0,1:T(8,128)(2,1)}) %all-gather.9.cloned.1.call-update) | async-done | bytes 9437200 | tf_op jit(solution)/shard_map/all_gather | solution.py:79
  1449.6 16.9 %scatter_fusion = f32[16,128,8,128]{3,1,2,0:T(8,128)} fusion(f32[16,128,8,128]{3,1,2,0:T(8,128)} %copy.42, s32[72]{0:T(128)S(1)} %reshape.361, f32[72,128,128]{2,1,0:T(8,128)} %bitcast.266), kind=kCustom, calls=%fused_computation.8 | custom fusion | flops 1179648 | bytes 14156352 | tf_op jit(solution)/shard_map/scatter-add | solution.py:94
  1466.5 17.0 %scatter_fusion.1 = f32[16,128,8,128]{3,1,2,0:T(8,128)} fusion(f32[16,128,8,128]{3,1,2,0:T(8,128)} %scatter_fusion, s32[72]{0:T(128)S(1)} %reshape.367, f32[72,128,128]{2,1,0:T(8,128)} %bitcast.267), kind=kCustom, calls=%fused_computation.9 | custom fusion | flops 1179648 | bytes 14156352 | tf_op jit(solution)/shard_map/scatter-add | solution.py:94
  1483.5 17.0 %scatter_fusion.2 = f32[16,128,8,128]{3,1,2,0:T(8,128)} fusion(f32[16,128,8,128]{3,1,2,0:T(8,128)} %scatter_fusion.1, s32[72]{0:T(128)S(1)} %reshape.373, f32[72,128,128]{2,1,0:T(8,128)} %bitcast.268), kind=kCustom, calls=%fused_computation.10 | custom fusion | flops 1179648 | bytes 14156352 | tf_op jit(solution)/shard_map/scatter-add | solution.py:94
  1500.4 16.9 %scatter_fusion.3 = f32[16,128,8,128]{3,1,2,0:T(8,128)} fusion(f32[16,128,8,128]{3,1,2,0:T(8,128)} %scatter_fusion.2, s32[72]{0:T(128)S(1)} %reshape.379, f32[72,128,128]{2,1,0:T(8,128)} %bitcast.269), kind=kCustom, calls=%fused_computation.11 | custom fusion | flops 1179648 | bytes 14156352 | tf_op jit(solution)/shard_map/scatter-add | solution.py:94
  1517.3 13.1 copy.49
  (312 shorter events, 641.0 us)
Async XLA Ops:
  7.2 175.8 %all-gather.5.cloned.1.call-start = ((), (), s32[]{:S(2)}) async-start(), calls=%async_computation | async-start | bytes 4325376 | tf_op jit(solution)/shard_map/all_gather | solution.py:33
  8.8 811.7 %all-gather.7.cloned.1.call-start = ((), (), s32[]{:S(2)}) async-start(), calls=%async_computation.1 | async-start | bytes 4325376 | tf_op jit(solution)/shard_map/all_gather | solution.py:33
  10.2 33.9 %collective-permute-start = (f32[2048,128]{1,0:T(8,128)S(1)}, f32[2048,128]{1,0:T(8,128)}, u32[]{:S(2)}, u32[]{:S(2)}) collective-permute-start(f32[2048,128]{1,0:T(8,128)S(1)} %slice.455), channel_id=1, source_target_pairs={{0,1},{1,0},{2,3},{3,2},{4,5},{5,4},{6,7},{7,6},{8,9},{9,8},{10,11... | collective-permute-start | bytes 3145736 | tf_op jit(solution)/shard_map/ppermute | solution.py:12
  45.8 58.4 %collective-permute-start.1 = (f32[2048,256]{1,0:T(8,128)S(1)}, f32[2048,256]{1,0:T(8,128)}, u32[]{:S(2)}, u32[]{:S(2)}) collective-permute-start(f32[2048,256]{1,0:T(8,128)S(1)} %maximum_select_fusion.10), channel_id=1, source_target_pairs={{0,2},{1,3},{2,0},{3,1},{4,6},{5,7},{6,4},{7,5},{8,10},{9,11},{10,... | collective-permute-start | bytes 6291464 | tf_op jit(solution)/shard_map/ppermute | solution.py:12
  109.1 440.4 %collective-permute-start.2 = (f32[2048,512]{1,0:T(8,128)}, f32[2048,512]{1,0:T(8,128)}, u32[]{:S(2)}, u32[]{:S(2)}) collective-permute-start(f32[2048,512]{1,0:T(8,128)} %maximum_select_fusion.4), channel_id=1, source_target_pairs={{0,4},{1,5},{2,6},{3,7},{4,0},{5,1},{6,2},{7,3},{8,12},{9,13},{10,... | collective-permute-start | bytes 12582920 | tf_op jit(solution)/shard_map/ppermute | solution.py:12
  185.2 3.7 slice-start
  214.0 2.0 copy-start.2
  526.1 4.3 copy-start
  580.6 2.1 copy-start.5
  582.6 33.7 %collective-permute-start.3 = (bf16[896,1024]{1,0:T(8,128)(2,1)S(1)}, bf16[896,1024]{1,0:T(8,128)(2,1)}, u32[]{:S(2)}, u32[]{:S(2)}) collective-permute-start(bf16[896,1024]{1,0:T(8,128)(2,1)S(1)} %bitcast.275), channel_id=1, source_target_pairs={{0,8},{1,9},{2,10},{3,11},{4,12},{5,13},{6,14},{7,15},{8,0},{9,1},... | collective-permute-start | bytes 5505032 | tf_op jit(solution)/shard_map/ppermute | solution.py:12
  617.9 28.5 %collective-permute-start.4 = (bf16[896,1024]{1,0:T(8,128)(2,1)}, bf16[896,1024]{1,0:T(8,128)(2,1)S(1)}, u32[]{:S(2)}, u32[]{:S(2)}) collective-permute-start(bf16[896,1024]{1,0:T(8,128)(2,1)} %broadcast_select_fusion), channel_id=1, source_target_pairs={{0,16},{1,17},{2,18},{3,19},{4,20},{5,21},{6,22},{7,23},{8,24},{9,... | collective-permute-start | bytes 5505032 | tf_op jit(solution)/shard_map/ppermute | solution.py:12
  654.4 2.7 copy-start.7
  657.8 708.4 %all-gather.9.cloned.1.call-start = ((), (), s32[]{:S(2)}) async-start(), calls=%async_computation.2 | async-start | bytes 11796480 | tf_op jit(solution)/shard_map/all_gather | solution.py:79
  659.1 30.3 %collective-permute-start.5 = (f32[1792,128]{0,1:T(8,128)S(1)}, f32[1792,128]{0,1:T(8,128)S(1)}, u32[]{:S(2)}, u32[]{:S(2)}) collective-permute-start(f32[1792,128]{0,1:T(8,128)S(1)} %slice.483), channel_id=1, source_target_pairs={{0,1},{1,0},{2,3},{3,2},{4,5},{5,4},{6,7},{7,6},{8,9},{9,8},{10,11... | collective-permute-start | bytes 2752520 | tf_op jit(solution)/shard_map/ppermute | solution.py:12
  689.6 30.9 %collective-permute-start.6 = (f32[1792,256]{0,1:T(8,128)S(1)}, f32[1792,256]{0,1:T(8,128)}, u32[]{:S(2)}, u32[]{:S(2)}) collective-permute-start(f32[1792,256]{0,1:T(8,128)S(1)} %maximum_select_fusion.11), channel_id=1, source_target_pairs={{0,2},{1,3},{2,0},{3,1},{4,6},{5,7},{6,4},{7,5},{8,10},{9,11},{10,... | collective-permute-start | bytes 5505032 | tf_op jit(solution)/shard_map/ppermute | solution.py:12
  724.7 465.2 %collective-permute-start.7 = (f32[1792,512]{0,1:T(8,128)}, f32[1792,512]{0,1:T(8,128)}, u32[]{:S(2)}, u32[]{:S(2)}) collective-permute-start(f32[1792,512]{0,1:T(8,128)} %maximum_select_fusion.9), channel_id=1, source_target_pairs={{0,4},{1,5},{2,6},{3,7},{4,0},{5,1},{6,2},{7,3},{8,12},{9,13},{10,... | collective-permute-start | bytes 11010056 | tf_op jit(solution)/shard_map/ppermute | solution.py:12
  832.7 1.6 copy-start.4
  853.6 1.9 copy-start.3
  1166.5 4.3 copy-start.1
  1189.3 101.3 %slice-start.1 = ((s8[6422528]{0:T(1024)(128)(4,1)}), s8[4194304]{0:T(1024)(128)(4,1)S(1)}, s32[]{:S(2)}) async-start(s8[6422528]{0:T(1024)(128)(4,1)} %bitcast.282), calls=%async_computation.4 | async-start | bytes 8388608
  1189.9 100.7 %slice-start.2 = ((s8[6422528]{0:T(1024)(128)(4,1)}), s8[2228224]{0:T(1024)(128)(4,1)S(1)}, s32[]{:S(2)}) async-start(s8[6422528]{0:T(1024)(128)(4,1)} %bitcast.282), calls=%async_computation.5 | async-start | bytes 4456448
  1240.7 49.8 %copy-start.6 = (bf16[1792,1024]{1,0:T(8,128)(2,1)}, bf16[1792,1024]{1,0:T(8,128)(2,1)S(1)}, u32[]{:S(2)}) copy-start(bf16[1792,1024]{1,0:T(8,128)(2,1)S(1)} %fusion.18) | copy-start | bytes 11010052
  1240.9 28.3 %collective-permute-start.8 = (bf16[768,1024]{1,0:T(8,128)(2,1)S(1)}, bf16[768,1024]{1,0:T(8,128)(2,1)S(1)}, u32[]{:S(2)}, u32[]{:S(2)}) collective-permute-start(bf16[768,1024]{1,0:T(8,128)(2,1)S(1)} %bitcast.278), channel_id=1, source_target_pairs={{0,8},{1,9},{2,10},{3,11},{4,12},{5,13},{6,14},{7,15},{8,0},{9,1},... | collective-permute-start | bytes 4718600 | tf_op jit(solution)/shard_map/ppermute | solution.py:12
  1269.5 25.3 %copy-start.9 = (s32[4,48]{1,0:T(4,128)S(1)}, s32[4,48]{1,0:T(4,128)}, u32[]{:S(2)}) copy-start(s32[4,48]{1,0:T(4,128)} %param.18) | copy-start | bytes 2308
  1269.5 21.0 %collective-permute-start.9 = (bf16[768,1024]{1,0:T(8,128)(2,1)S(1)}, bf16[768,1024]{1,0:T(8,128)(2,1)S(1)}, u32[]{:S(2)}, u32[]{:S(2)}) collective-permute-start(bf16[768,1024]{1,0:T(8,128)(2,1)S(1)} %broadcast_select_fusion.1), channel_id=1, source_target_pairs={{0,16},{1,17},{2,18},{3,19},{4,20},{5,21},{6,22},{7,23},{8,24},{9,... | collective-permute-start | bytes 4718600 | tf_op jit(solution)/shard_map/ppermute | solution.py:12
  1305.4 5.8 copy-start.8
Sparse Core Ops, SparseCore 0:
  10.2 172.7 all-gather.4
  657.9 162.5 all-gather.6
  1294.9 71.2 all-gather.8
where the time goes:
time: 1560 us; the launch traced here: 1550 us
  other arithmetic  629 us (40%)
  waiting for transfers between devices  438 us (28%)
  local copies, waits for them, and re-layouts  237 us (15%)
  matrix products  187 us (12%)
  starting transfers between devices  28.2 us (2%)
  between operations  28 us (2%)
    another operation x61, other arithmetic, per_device(): lower_factor = jnp.linalg.cholesky(diagonal)  345 us
    ppermute x10, waiting for transfers between devices, from_partner(): lax.ppermute(value, axis, [(i, i ^ 1 << distance) for i in range(lax.axis...  221 us
    all_gather x2, waiting for transfers between devices, per_device(): everyone = lax.all_gather(corner, 'tile', axis=0, tiled=True)  169 us
    another operation x5, other arithmetic, per_device(): lax.linalg.triangular_solve(lower_factor, identity, left_side=True, lower...  167 us
    dot_general x2, matrix products, per_device(): jnp.dot(gathered, inverse.T, precision=lax.Precision.HIGHEST, preferred_e...  81.9 us
    mul x12, local copies, waits for them, and re-layouts, per_device(): weight * blocks  74 us
    scatter-add x4, other arithmetic, per_device(): accum.at[target_rows[:, None], :, target_cols[None, :], :]  67.7 us
    all_gather x1, waiting for transfers between devices, per_device(): arrived = lax.all_gather(contribution, 'front', axis=0, tiled=True)  47.8 us
  transfers between devices with their start and end apart: 13, of which 11 were waited for; matrix products, arithmetic and copies ran while one was open for 50% of the time, Pallas kernels for 0%

commit v1 on v0

v1 whole, which is shorter than its diff:
```python
import functools

import jax
import jax.numpy as jnp
from jax import lax
from jax.experimental import pallas as pl
from jax.experimental.pallas import tpu as pltpu
from jax.sharding import PartitionSpec as P

BLK = 128
F32 = jnp.float32
BF16 = jnp.bfloat16
NN = (((1,), (0,)), ((), ()))
NT = (((1,), (1,)), ((), ()))


def dot(a, b, dims):
    return lax.dot_general(a, b, dims, preferred_element_type=F32)


def dot_exact(a, b, dims):
    return lax.dot_general(a, b, dims, precision=lax.Precision.HIGHEST, preferred_element_type=F32)


def split(x):
    hi = x.astype(BF16)
    return hi, (x - hi.astype(F32)).astype(BF16)


def dot3(a, b, dims):
    return dot(a[0], b[0], dims) + (dot(a[0], b[1], dims) + dot(a[1], b[0], dims))


def lane_of(x, lane):
    return jnp.broadcast_to(x[:, lane : lane + 1], (8, BLK))


def row_of(x, row):
    return jnp.broadcast_to(x[row : row + 1, :], (8, BLK))


def factor_block(rows, out_ref, out_row, out_col):
    S = list(rows)
    lanes = lax.broadcasted_iota(jnp.int32, (8, BLK), 1)
    subs = lax.broadcasted_iota(jnp.int32, (8, BLK), 0)
    G = [(lanes == subs + 8 * v).astype(F32) for v in range(16)]
    for v0 in range(16):
        C = {v: [lane_of(S[v], 8 * v0 + j) for j in range(8)] for v in range(v0, 16)}
        d = [[row_of(C[v0][j], i) if i >= j else None for j in range(8)] for i in range(8)]
        Rs = [row_of(S[v0], i) for i in range(8)]
        Rg = [row_of(G[v0], i) for i in range(8)]
        Cn = list(C[v0 + 1]) if v0 < 15 else None
        m = [[None] * 8 for _ in range(8)]
        Us, Ug = [None] * 8, [None] * 8
        wrows = None
        for j in range(8):
            rs = lax.rsqrt(d[j][j])
            p = rs * rs
            w = Rg[j] * rs
            wrows = w if j == 0 else jnp.where(subs == j, w, wrows)
            for i in range(j + 1, 8):
                m[i][j] = d[i][j] * p
            for i in range(j + 1, 8):
                for k in range(j + 1, i + 1):
                    d[i][k] = d[i][k] - m[i][j] * d[k][j]
            Us[j] = Rs[j] * p
            Ug[j] = Rg[j] * p
            if Cn is not None:
                S[v0 + 1] = S[v0 + 1] - Cn[j] * Us[j]
                G[v0 + 1] = G[v0 + 1] - Cn[j] * Ug[j]
            for i in range(j + 1, 8):
                Rs[i] = Rs[i] - m[i][j] * Rs[j]
                Rg[i] = Rg[i] - m[i][j] * Rg[j]
                if Cn is not None:
                    Cn[i] = Cn[i] - m[i][j] * Cn[j]
        out_ref[pl.ds(out_row + 8 * v0, 8), pl.ds(out_col, BLK)] = wrows
        if v0 < 14:
            for j in range(6, -1, -1):
                for i in range(j + 1, 8):
                    Us[j] = Us[j] - m[i][j] * Us[i]
                    Ug[j] = Ug[j] - m[i][j] * Ug[i]
            for v in range(v0 + 2, 16):
                for j in range(8):
                    S[v] = S[v] - C[v][j] * Us[j]
                    G[v] = G[v] - C[v][j] * Ug[j]


def chol_inverse(A, W, Ls):
    W[...] = jnp.zeros(W.shape, F32)

    def step(kb, _):
        r0 = pl.multiple_of(kb * BLK, BLK)
        rows = [A[pl.ds(pl.multiple_of(r0 + 8 * v, 8), 8), pl.ds(r0, BLK)] for v in range(16)]
        factor_block(rows, W, r0, r0)

        @pl.when(kb % 2 == 0)
        def _():
            r1 = pl.multiple_of(r0 + BLK, BLK)
            wkk = W[pl.ds(r0, BLK), pl.ds(r0, BLK)]
            low = dot_exact(A[pl.ds(r1, BLK), pl.ds(r0, BLK)], wkk, NT)
            Ls[...] = low
            A[pl.ds(r1, BLK), pl.ds(r1, BLK)] -= dot_exact(low, low, NT)

        @pl.when(kb % 2 == 1)
        def _():
            q = pl.multiple_of(r0 - BLK, BLK)
            t = dot_exact(Ls[...], W[pl.ds(q, BLK), pl.ds(q, BLK)], NN)
            W[pl.ds(r0, BLK), pl.ds(q, BLK)] = -dot_exact(W[pl.ds(r0, BLK), pl.ds(r0, BLK)], t, NN)

        for c in range(4):
            @pl.when(kb == 2 * c + 1)
            def _():
                lo, hi = 256 * c, 256 * (c + 1)
                wd = W[lo:hi, lo:hi]
                if c > 0:
                    W[lo:hi, :lo] = dot_exact(wd, W[lo:hi, :lo], NN)
                if c < 3:
                    low = dot_exact(A[hi:, lo:hi], wd, NT)
                    for n in range(c + 1, 4):
                        a, b = 256 * n, 256 * (n + 1)
                        A[a:, a:b] -= dot_exact(low[a - hi :], low[a - hi : b - hi], NT)
                    W[hi:, lo:hi] = -dot_exact(low, wd, NN)
                    if c > 0:
                        W[hi:, :lo] -= dot_exact(low, W[lo:hi, :lo], NN)

        return 0

    lax.fori_loop(0, 8, step, 0)


VMEM = pl.BlockSpec(memory_space=pltpu.VMEM)
PARAMS = pltpu.CompilerParams(vmem_limit_bytes=56 * 2**20)


def cost(flops, data):
    return pl.CostEstimate(flops=flops, bytes_accessed=data, transcendentals=0)


def position():
    tile = lax.axis_index("tile")
    return tile // 8, tile % 8


def times_inverse_t(x, w, put):
    for n in range(4):
        a, b = 256 * n, 256 * (n + 1)
        put(n, dot3((x[0][:, :b], x[1][:, :b]), (w[0][a:b, :b], w[1][a:b, :b]), NT))


def inverse_times(w, x, put):
    for n in range(4):
        a, b = 256 * n, 256 * (n + 1)
        put(n, dot3((w[0][a:b, :b], w[1][a:b, :b]), (x[0][:b], x[1][:b]), NN))


def store_split(hi, lo, index, x):
    h, l = split(x)
    hi[index] = h
    lo[index] = l


def own_columns(left, W, row, col, out, at):
    wc = W[pl.ds(pl.multiple_of(col * BLK, BLK), BLK), :]
    own = dot_exact(left, wc, NT)
    for m in range(2):
        keep = 4 * m + (row + 3) % 4 >= col
        out[m * BLK : (m + 1) * BLK, at : at + BLK] = jnp.where(keep, own[m * BLK : (m + 1) * BLK], 0.0).astype(BF16)


def first_kernel(g, whi, wlo, top, A, W, Ls):
    row, col = position()
    for i in range(8):
        for j in range(8):
            A[i * BLK : (i + 1) * BLK, j * BLK : (j + 1) * BLK] = g[8 * ((i + 1) % 4) + j, (i // 4) * BLK : (i // 4 + 1) * BLK, :]
    chol_inverse(A, W, Ls)
    store_split(whi, wlo, ..., W[...])
    top[...] = jnp.zeros(top.shape, BF16)
    left = jnp.concatenate([g[8 * row + j] for j in range(8)], 1)
    own_columns(left, W, row, col, top, 0)


def second_kernel(g, w0hi, w0lo, low, whi, wlo, top, A, W, Ls, xhi, xlo, keep):
    row, col = position()
    for i in range(8):
        for j in range(8):
            src = g[8 * ((i + 1) % 4) + j, (i // 4) * BLK : (i // 4 + 1) * BLK, :]
            at = slice(i * BLK, (i + 1) * BLK), slice(j * BLK, (j + 1) * BLK)
            store_split(xhi, xlo, at, src[:, :BLK])
            A[at] = src[:, BLK:]

    def put(n, x):
        low[:, 256 * n : 256 * (n + 1)] = x.astype(BF16)

    times_inverse_t((xhi, xlo), (w0hi, w0lo), put)
    for n in range(4):
        a, b = 256 * n, 256 * (n + 1)
        A[a:, a:b] -= dot(low[a:, :], low[a:b, :], NT)
    for m in range(2):
        at = pl.multiple_of((4 * m + (row + 3) % 4) * BLK, BLK)
        keep[m * BLK : (m + 1) * BLK, :] = A[pl.ds(at, BLK), :]
        top[m * BLK : (m + 1) * BLK, :BLK] = low[pl.ds(at, BLK), pl.ds(pl.multiple_of(col * BLK, BLK), BLK)]
    chol_inverse(A, W, Ls)
    store_split(whi, wlo, ..., W[...])
    own_columns(keep[...], W, row, col, top, BLK)


def rows_kernel(panel, *refs):
    pieces, refs = refs[:8], refs[8:]
    row, col = position()
    if panel == 0:
        whi, wlo, out, x = refs
    else:
        whi, wlo, low, first, out, x = refs
    for k in range(8):
        x[:, pl.ds(pl.multiple_of((col ^ k) * BLK, BLK), BLK)] = pieces[k][:, panel * BLK : (panel + 1) * BLK]
    v = x[...]
    if panel == 1:
        v = v - dot(first[...], low[...], NT)

    def put(n, y):
        out[:, 256 * n : 256 * (n + 1)] = y.astype(BF16)

    times_inverse_t(split(v), (whi, wlo), put)


def columns_kernel(*refs):
    pieces = refs[:4]
    w0hi, w0lo, w1hi, w1lo, low, t0, t1, xhi, xlo, y = refs[4:]
    row, _ = position()
    for k in range(4):
        place = ((row ^ k) + 3) % 4
        for m in range(4):
            src = pieces[k][m * BLK : (m + 1) * BLK, :]
            at = pl.ds(pl.multiple_of((4 * (m % 2) + place) * BLK, BLK), BLK)
            if m < 2:
                store_split(xhi, xlo, (at, slice(None)), src)
            else:
                y[at, :] = src

    def put(t):
        def go(n, v):
            t[256 * n : 256 * (n + 1), :] = v.astype(BF16)

        return go

    inverse_times((w0hi, w0lo), (xhi, xlo), put(t0))
    for n in range(4):
        at = slice(256 * n, 256 * (n + 1)), slice(None)
        store_split(xhi, xlo, at, y[at] - dot(low[at], t0[...], NN))
    inverse_times((w1hi, w1lo), (xhi, xlo), put(t1))


def update_kernel(l0, l1, t0, t1, a, out, factor):
    _, col = position()
    out[...] = (a[...] - (dot(l0[...], t0[...], NN) + dot(l1[...], t1[...], NN))).astype(BF16)

    @pl.when(pl.program_id(1) == 0)
    def _():
        at = pl.ds(pl.multiple_of(col * BLK, BLK), BLK)
        factor[:, :BLK] = l0[:, at]
        factor[:, BLK:] = l1[:, at]


def merge_kernel(rows, cols, parent, *refs):
    blocks, out = refs[:4], refs[4]
    i = pl.program_id(0)
    out[...] = parent[...].astype(F32)
    for g in range(4):
        @pl.when(rows[g, i] >= 0)
        def _():
            for j in range(8):
                b = cols[g, j]

                @pl.when(b >= 0)
                def _():
                    at = pl.ds(pl.multiple_of(b * BLK, BLK), BLK)
                    out[:, j * BLK : (j + 1) * BLK] += blocks[g][0, :, at].astype(F32)


def per_device(fronts, parents, parent_of, block_map):
    tile = lax.axis_index("tile")
    row, col = tile // 8, tile % 8
    my_front = lax.axis_index("front")
    a = fronts[0, 0]
    big = jax.ShapeDtypeStruct((1024, 1024), BF16)
    square = pltpu.VMEM((1024, 1024), F32)
    half = pltpu.VMEM((1024, 1024), BF16)
    block = pltpu.VMEM((BLK, BLK), F32)
    top_shape = jax.ShapeDtypeStruct((256, 256), BF16)

    place_r = jnp.arange(12) * 4 + (row + 3) % 4
    place_c = jnp.arange(6) * 8 + col
    at_rows = block_map[:, place_r] // 4
    at_cols = block_map[:, place_c] // 8
    mine = (parent_of == my_front)[:, None]
    hit_r = (at_rows[:, :, None] == jnp.arange(16)) & mine[:, :, None]
    hit_c = at_cols[:, :, None] == jnp.arange(8)
    from_rows = jnp.max(jnp.where(hit_r, jnp.arange(12)[:, None], -1), axis=1).astype(jnp.int32)
    from_cols = jnp.max(jnp.where(hit_c, jnp.arange(6)[:, None], -1), axis=1).astype(jnp.int32)

    g0 = lax.all_gather(a[:256, :BLK], "tile", axis=0)
    g0, a = lax.optimization_barrier((g0, a))
    g1 = lax.all_gather(a[256:512, :256], "tile", axis=0)

    def swap(x, k):
        return lax.ppermute(x, "tile", [(i, i ^ k) for i in range(32)])

    trail = a[512:, :256].reshape(8, 192, 256)
    pieces = [lax.dynamic_index_in_dim(trail, col ^ k, 0, keepdims=False) for k in range(8)]
    pieces = pieces[:1] + [swap(pieces[k], k) for k in range(1, 8)]
    side = a[:512, 256:]
    sides = [side] + [swap(side, 8 * k) for k in range(1, 4)]

    w0hi, w0lo, top0 = pl.pallas_call(
        first_kernel,
        out_shape=(big, big, top_shape),
        in_specs=[VMEM],
        out_specs=(VMEM,) * 3,
        scratch_shapes=[square, square, block],
        compiler_params=PARAMS,
        cost_estimate=cost(50_000_000_000, 8_000_000),
        name="first_panel",
    )(g0)
    first = pl.pallas_call(
        functools.partial(rows_kernel, 0),
        out_shape=jax.ShapeDtypeStruct((192, 1024), BF16),
        in_specs=[VMEM] * 10,
        out_specs=VMEM,
        scratch_shapes=[pltpu.VMEM((192, 1024), F32)],
        compiler_params=PARAMS,
        cost_estimate=cost(1_200_000_000, 6_000_000),
        name="first_rows",
    )(*pieces, w0hi, w0lo)
    groups = [[8 * r + c for c in range(8)] for r in range(4)]
    l0 = lax.all_gather(first, "tile", axis=0, tiled=True, axis_index_groups=groups)
    low, w1hi, w1lo, top1 = pl.pallas_call(
        second_kernel,
        out_shape=(big, big, big, top_shape),
        in_specs=[VMEM] * 3,
        out_specs=(VMEM,) * 4,
        scratch_shapes=[square, square, block, half, half, pltpu.VMEM((256, 1024), F32)],
        compiler_params=PARAMS,
        cost_estimate=cost(60_000_000_000, 16_000_000),
        name="second_panel",
    )(g1, w0hi, w0lo)
    second = pl.pallas_call(
        functools.partial(rows_kernel, 1),
        out_shape=jax.ShapeDtypeStruct((192, 1024), BF16),
        in_specs=[VMEM] * 12,
        out_specs=VMEM,
        scratch_shapes=[pltpu.VMEM((192, 1024), F32)],
        compiler_params=PARAMS,
        cost_estimate=cost(1_700_000_000, 8_000_000),
        name="second_rows",
    )(*pieces, w1hi, w1lo, low, first)
    l1 = lax.all_gather(second, "tile", axis=0, tiled=True, axis_index_groups=groups)
    wide = jax.ShapeDtypeStruct((1024, 768), BF16)
    t0, t1 = pl.pallas_call(
        columns_kernel,
        out_shape=(wide, wide),
        in_specs=[VMEM] * 9,
        out_specs=(VMEM,) * 2,
        scratch_shapes=[pltpu.VMEM((1024, 768), BF16)] * 2 + [pltpu.VMEM((1024, 768), F32)],
        compiler_params=PARAMS,
        cost_estimate=cost(12_000_000_000, 18_000_000),
        name="column_rows",
    )(*sides, w0hi, w0lo, w1hi, w1lo, low)
    contribution, lower = pl.pallas_call(
        update_kernel,
        grid=(3, 3),
        out_shape=(
            jax.ShapeDtypeStruct((1536, 768), BF16),
            jax.ShapeDtypeStruct((1536, 256), BF16),
        ),
        in_specs=[
            pl.BlockSpec((512, 1024), lambda i, j: (i, 0)),
            pl.BlockSpec((512, 1024), lambda i, j: (i, 0)),
            pl.BlockSpec((1024, 256), lambda i, j: (0, j)),
            pl.BlockSpec((1024, 256), lambda i, j: (0, j)),
            pl.BlockSpec((512, 256), lambda i, j: (i + 1, j + 1)),
        ],
        out_specs=(
            pl.BlockSpec((512, 256), lambda i, j: (i, j)),
            pl.BlockSpec((512, 256), lambda i, j: (i, 0)),
        ),
        compiler_params=PARAMS,
        cost_estimate=cost(4_900_000_000, 17_000_000),
        name="update",
    )(l0, l1, t0, t1, a)
    factor = jnp.concatenate([top0, top1, lower], 0)
    arrived = lax.all_gather(contribution, "front", axis=0)

    def child(g):
        return pl.BlockSpec((1, BLK, 768), lambda i, rows, cols: (g, jnp.maximum(rows[g, i], 0), 0))

    merged = pl.pallas_call(
        merge_kernel,
        grid_spec=pltpu.PrefetchScalarGridSpec(
            num_scalar_prefetch=2,
            grid=(16,),
            in_specs=[pl.BlockSpec((BLK, 1024), lambda i, rows, cols: (i, 0))] + [child(g) for g in range(4)],
            out_specs=pl.BlockSpec((BLK, 1024), lambda i, rows, cols: (i, 0)),
        ),
        out_shape=jax.ShapeDtypeStruct((2048, 1024), F32),
        compiler_params=PARAMS,
        cost_estimate=cost(10_000_000, 22_000_000),
        name="merge",
    )(from_rows, from_cols, parents[0, 0], *[arrived] * 4)
    return factor[None, None], merged[None, None]


def solution(mesh):
    return jax.shard_map(
        per_device,
        mesh=mesh,
        in_specs=(P("front", "tile", None, None), P("front", "tile", None, None), P(), P()),
        out_specs=(P("front", "tile", None, None), P("front", "tile", None, None)),
        check_vma=False,
    )
```

time: 1560 us -> 628 us (0.40)
  other arithmetic: 629 us -> 2.37 us
  local copies, waits for them, and re-layouts: 237 us -> 11 us
  matrix products: 187 us -> 0 us
  Pallas kernels: 0 us -> 183 us
  waiting for transfers between devices: 438 us -> 380 us
    another operation x66 -> x0, other arithmetic: 513 us -> none  [the longest x61 345 us: per_device(): lower_factor = jnp.linalg.cholesky(diagonal)]
    pallas_call x0 -> x7, Pallas kernels: none -> 183 us  [the longest x1 68.5 us: per_device(): pl.pallas_call(second_kernel, out_shape=(big, big, big, top_shape), in_sp...]
    ppermute x10, waiting for transfers between devices: 221 us -> 77.7 us  [swap(): return lax.ppermute(x, 'tile', [(i, i ^ k) for i in range(32)])]
    dot_general x4 -> x0, matrix products: 94.1 us -> none  [the longest x2 81.9 us: per_device(): jnp.dot(gathered, inverse.T, precision=lax.Precision.HIGHEST, preferred_e...]
    another operation x58 -> x0, matrix products: 92.8 us -> none  [the longest x30 46.5 us: per_device(): lax.linalg.triangular_solve(lower_factor, identity, left_side=True, lower...]
    all_gather x3 -> x5, waiting for transfers between devices: 217 us -> 302 us  [the longest x1 154 us: per_device(): g0 = lax.all_gather(a[:256, :BLK], 'tile', axis=0)]
    mul x12 -> x0, local copies, waits for them, and re-layouts: 74 us -> none  [per_device(): weight * blocks]
    scatter-add x4 -> x0, other arithmetic: 67.7 us -> none  [per_device(): accum.at[target_rows[:, None], :, target_cols[None, :], :]]
  transfers between devices with their start and end apart: 13 -> 15, of which waited for: 11 -> 5; matrix products, arithmetic and copies ran while one was open for 50% -> 1% of each run, Pallas kernels for 0% -> 25%
where the time goes in v1:
time: 628 us; the launch traced here: 623 us
  waiting for transfers between devices  380 us (61%)
  Pallas kernels  183 us (29%)
  starting transfers between devices  32.2 us (5%)
  between operations  14.2 us (2%)
  local copies, waits for them, and re-layouts  11 us (2%)
    all_gather x1, waiting for transfers between devices, per_device(): g0 = lax.all_gather(a[:256, :BLK], 'tile', axis=0)  154 us
    all_gather x1, waiting for transfers between devices, per_device(): g1 = lax.all_gather(a[256:512, :256], 'tile', axis=0)  82.2 us
    ppermute x10, waiting for transfers between devices, swap(): return lax.ppermute(x, 'tile', [(i, i ^ k) for i in range(32)])  77.7 us
    pallas_call x1, Pallas kernels, per_device(): pl.pallas_call(second_kernel, out_shape=(big, big, big, top_shape), in_sp...  68.5 us
    all_gather x1, waiting for transfers between devices, per_device(): arrived = lax.all_gather(contribution, 'front', axis=0)  66.5 us
    pallas_call x1, Pallas kernels, per_device(): pl.pallas_call(first_kernel, out_shape=(big, big, top_shape), in_specs=[V...  59.9 us
    ppermute x10, starting transfers between devices, swap(): return lax.ppermute(x, 'tile', [(i, i ^ k) for i in range(32)])  32 us
    pallas_call x1, Pallas kernels, per_device(): pl.pallas_call(columns_kernel, out_shape=(wide, wide), in_specs=[VMEM] *...  16.2 us
  transfers between devices with their start and end apart: 15, of which 5 were waited for; matrix products, arithmetic and copies ran while one was open for 1% of the time, Pallas kernels for 25%

profile of v1, /device:TPU:16, one launch (start us, length us, event | category | flops | bytes accessed | tf_op | source)
XLA Modules:
  0.0 622.7 jit_solution(8750884451539606163)
XLA Ops:
  7.2 1.6 slice.20
  8.9 153.6 %all-gather.13.cloned.1.call-done = f32[8192,128]{1,0:T(8,128)} async-done(((f32[256,128]{1,0:T(8,128)}), f32[8192,128]{1,0:T(8,128)}) %all-gather.13.cloned.1.call-update) | async-done | bytes 4194320 | tf_op jit(solution)/shard_map/all_gather | solution.py:301
  162.4 1.7 slice.13
  164.2 1.5 slice.14
  165.7 0.9 dynamic-slice_bitcast_fusion
  166.6 5.9 collective-permute-start.1
  172.6 0.6 collective-permute-start.2
  173.1 7.2 %collective-permute-start.3 = (f32[192,256]{1,0:T(8,128)S(1)}, f32[192,256]{1,0:T(8,128)S(1)}, u32[]{:S(2)}, u32[]{:S(2)}) collective-permute-start(f32[192,256]{1,0:T(8,128)S(1)} %get-tuple-element.31), channel_id=1, source_target_pairs={{0,4},{1,5},{2,6},{3,7},{4,0},{5,1},{6,2},{7,3},{8,12},{9,13},{10,... | collective-permute-start | bytes 589832 | tf_op jit(solution)/shard_map/ppermute | solution.py:306
  180.3 5.6 collective-permute-start.5
  185.9 59.9 %first_panel.1 = (bf16[1024,1024]{1,0:T(8,128)(2,1)}, bf16[1024,1024]{1,0:T(8,128)(2,1)}, bf16[256,256]{1,0:T(8,128)(2,1)}) custom-call(f32[32,256,128]{2,1,0:T(8,128)} %bitcast.74), custom_call_target="tpu_custom_call" | custom-call | flops 49999998976 | bytes 8000000 | tf_op jit(solution)/shard_map/first_panel/pallas_call | solution.py:314
  245.9 0.6 copy-done.3
  246.6 0.1 copy-done.5
  246.8 5.1 first_rows.1.refs_11_
  251.9 82.2 %all-gather.15.cloned.1.call-done = f32[8192,256]{1,0:T(8,128)} async-done(((f32[256,256]{1,0:T(8,128)}), f32[8192,256]{1,0:T(8,128)}) %all-gather.15.cloned.1.call-update) | async-done | bytes 8388624 | tf_op jit(solution)/shard_map/all_gather | solution.py:303
  334.2 68.5 %second_panel.1 = (bf16[1024,1024]{1,0:T(8,128)(2,1)}, bf16[1024,1024]{1,0:T(8,128)(2,1)}, bf16[1024,1024]{1,0:T(8,128)(2,1)}, bf16[256,256]{1,0:T(8,128)(2,1)}) custom-call(f32[32,256,256]{2,1,0:T(8,128)} %bitcast.73, bf16[1024,1024]{1,0:T(8,128)(2,1)} %get-tuple-element.18.w0hi.refs_8_.refs_4_, bf16[1024,1024]{1,0:T(8,128)(2,1)} %get-tuple-element.19.w0lo.refs_9_.refs_5_), custom_call_target="tpu_custom_call" | custom-call | flops 60000002048 | bytes 16000000 | tf_op jit(solution)/shard_map/second_panel/pallas_call | solution.py:336
  402.7 6.3 %second_rows.1 = bf16[192,1024]{1,0:T(8,128)(2,1)} custom-call(f32[192,256]{1,0:T(8,128)} %get-tuple-element.35.refs_0_, f32[192,256]{1,0:T(8,128)} %copy-done.1, f32[192,256]{1,0:T(8,128)} %copy-done.2, f32[192,256]{1,0:T(8,128)} %copy-done.3, f32[192,256]{1,0:T(8,128)} %copy-done.4, f32[192,256]{1,0:T(8,128)} %copy-done.5, f32[192,256]{1,0:T(8,128)} %copy-done.6, ...), custom_call_target="tpu_custom_call" | custom-call | flops 1700000000 | bytes 8000000 | tf_op jit(solution)/shard_map/second_rows/pallas_call | solution.py:346
  409.0 1.5 slice.15.refs_0_
  410.6 11.1 %collective-permute-start.7 = (f32[512,768]{1,0:T(8,128)S(1)}, f32[512,768]{1,0:T(8,128)S(1)}, u32[]{:S(2)}, u32[]{:S(2)}) collective-permute-start(f32[512,768]{1,0:T(8,128)S(1)} %slice.15.refs_0_), channel_id=1, source_target_pairs={{0,8},{1,9},{2,10},{3,11},{4,12},{5,13},{6,14},{7,15},{8,0},{9,1},... | collective-permute-start | bytes 4718600 | tf_op jit(solution)/shard_map/ppermute | solution.py:306
  421.7 1.5 collective-permute-start.9
  423.2 60.7 %collective-permute-done.7.refs_1_ = f32[512,768]{1,0:T(8,128)S(1)} collective-permute-done((f32[512,768]{1,0:T(8,128)S(1)}, f32[512,768]{1,0:T(8,128)S(1)}, u32[]{:S(2)}, u32[]{:S(2)}) %collective-permute-start.7) | collective-permute-done | bytes 1572896 | tf_op jit(solution)/shard_map/ppermute | solution.py:306
  484.0 16.9 %collective-permute-done.9.refs_3_ = f32[512,768]{1,0:T(8,128)S(1)} collective-permute-done((f32[512,768]{1,0:T(8,128)S(1)}, f32[512,768]{1,0:T(8,128)S(1)}, u32[]{:S(2)}, u32[]{:S(2)}) %collective-permute-start.9) | collective-permute-done | bytes 1572896 | tf_op jit(solution)/shard_map/ppermute | solution.py:306
  500.9 1.2 copy-done.14
  502.1 16.2 %column_rows.1 = (bf16[1024,768]{1,0:T(8,128)(2,1)}, bf16[1024,768]{1,0:T(8,128)(2,1)}) custom-call(f32[512,768]{1,0:T(8,128)} %copy-done, f32[512,768]{1,0:T(8,128)} %copy-done.12, f32[512,768]{1,0:T(8,128)} %copy-done.13, f32[512,768]{1,0:T(8,128)} %copy-done.14, bf16[1024,1024]{1,0:T(8,128)(2,1)} %get-tuple-element.18.w0hi.refs_8_.refs_4_, ...), custom_call_target="tpu_custom_call" | custom-call | flops 12000000000 | bytes 18000000 | tf_op jit(solution)/shard_map/column_rows/pallas_call | solution.py:358
  518.4 13.5 %update.1 = (bf16[1536,768]{1,0:T(8,128)(2,1)}, bf16[1536,256]{1,0:T(8,128)(2,1)}) custom-call(bf16[1536,1024]{1,0:T(8,128)(2,1)} %all-gather.9.cloned.1.call-done.l0, bf16[1536,1024]{1,0:T(8,128)(2,1)} %all-gather.11.cloned.1.call-done.l1, bf16[1024,768]{1,0:T(8,128)(2,1)} %get-tuple-element.24.t0, bf16[1024,768]{1,0:T(8,128)(2,1)} %get-tuple-element.25.t1, ...), custom_call_target="tpu_custom_call" | custom-call | flops 4899999744 | bytes 17000000 | tf_op jit(solution)/shard_map/update/pallas_call | solution.py:368
  531.9 0.6 copy-done.11
  532.6 0.6 gather_fusion
  533.2 0.6 gather_fusion.1
  533.8 0.7 select_reduce_fusion.1.cols
  534.5 0.6 select_reduce_fusion.rows
  535.1 1.0 maximum_bitcast_fusion
  536.1 66.5 %all-gather.17.cloned.1.call-done = bf16[6144,768]{1,0:T(8,128)(2,1)} async-done(((bf16[1536,768]{1,0:T(8,128)(2,1)}), bf16[6144,768]{1,0:T(8,128)(2,1)}) %all-gather.17.cloned.1.call-update) | async-done | bytes 9437200 | tf_op jit(solution)/shard_map/all_gather | solution.py:391
  602.7 13.3 %merge.1 = f32[2048,1024]{1,0:T(8,128)} custom-call(s32[4,16]{1,0:T(4,128)} %select_reduce_fusion.rows, s32[4,8]{1,0:T(4,128)} %select_reduce_fusion.1.cols, bf16[2048,1024]{1,0:T(8,128)(2,1)} %bitcast.67, bf16[4,1536,768]{2,1,0:T(8,128)(2,1)} %bitcast.61, bf16[4,1536,768]{2,1,0:T(8,128)(2,1)} %bitcast.62, bf16[4,1536,768]{2,1,0:T(8,128)(2,1)} %bitcast.63, ...), custom_call_target="tpu_custom_call" | custom-call | flops 10000000 | bytes 22000000 | tf_op jit(solution)/shard_map/merge/pallas_call | solution.py:396
  (60 shorter events, 0.8 us)
Async XLA Ops:
  7.2 155.3 %all-gather.13.cloned.1.call-start = ((), (), s32[]{:S(2)}) async-start(), calls=%async_computation.2 | async-start | bytes 4325376 | tf_op jit(solution)/shard_map/all_gather | solution.py:301
  8.8 325.4 %all-gather.15.cloned.1.call-start = ((), (), s32[]{:S(2)}) async-start(), calls=%async_computation.3 | async-start | bytes 8650752 | tf_op jit(solution)/shard_map/all_gather | solution.py:303
  164.1 354.2 %all-gather.9.cloned.1.call-start = ((), (), s32[]{:S(2)}) async-start(), calls=%async_computation | async-start | bytes 3538944 | tf_op jit(solution)/shard_map/all_gather | solution.py:335
  166.6 13.7 %collective-permute-start = (f32[192,256]{1,0:T(8,128)S(1)}, f32[192,256]{1,0:T(8,128)S(1)}, u32[]{:S(2)}, u32[]{:S(2)}) collective-permute-start(f32[192,256]{1,0:T(8,128)S(1)} %get-tuple-element.34), channel_id=1, source_target_pairs={{0,1},{1,0},{2,3},{3,2},{4,5},{5,4},{6,7},{7,6},{8,9},{9,8},{10,11... | collective-permute-start | bytes 589832 | tf_op jit(solution)/shard_map/ppermute | solution.py:306
  166.6 19.3 %collective-permute-start.1 = (f32[192,256]{1,0:T(8,128)S(1)}, f32[192,256]{1,0:T(8,128)S(1)}, u32[]{:S(2)}, u32[]{:S(2)}) collective-permute-start(f32[192,256]{1,0:T(8,128)S(1)} %get-tuple-element.33), channel_id=1, source_target_pairs={{0,2},{1,3},{2,0},{3,1},{4,6},{5,7},{6,4},{7,5},{8,10},{9,11},{10,... | collective-permute-start | bytes 589832 | tf_op jit(solution)/shard_map/ppermute | solution.py:306
  172.6 73.3 %collective-permute-start.2 = (f32[192,256]{1,0:T(8,128)S(1)}, f32[192,256]{1,0:T(8,128)S(1)}, u32[]{:S(2)}, u32[]{:S(2)}) collective-permute-start(f32[192,256]{1,0:T(8,128)S(1)} %get-tuple-element.32), channel_id=1, source_target_pairs={{0,3},{1,2},{2,1},{3,0},{4,7},{5,6},{6,5},{7,4},{8,11},{9,10},{10,... | collective-permute-start | bytes 589832 | tf_op jit(solution)/shard_map/ppermute | solution.py:306
  173.1 72.7 %collective-permute-start.3 = (f32[192,256]{1,0:T(8,128)S(1)}, f32[192,256]{1,0:T(8,128)S(1)}, u32[]{:S(2)}, u32[]{:S(2)}) collective-permute-start(f32[192,256]{1,0:T(8,128)S(1)} %get-tuple-element.31), channel_id=1, source_target_pairs={{0,4},{1,5},{2,6},{3,7},{4,0},{5,1},{6,2},{7,3},{8,12},{9,13},{10,... | collective-permute-start | bytes 589832 | tf_op jit(solution)/shard_map/ppermute | solution.py:306
  180.3 65.5 %collective-permute-start.4 = (f32[192,256]{1,0:T(8,128)S(1)}, f32[192,256]{1,0:T(8,128)S(1)}, u32[]{:S(2)}, u32[]{:S(2)}) collective-permute-start(f32[192,256]{1,0:T(8,128)S(1)} %get-tuple-element.30), channel_id=1, source_target_pairs={{0,5},{1,4},{2,7},{3,6},{4,1},{5,0},{6,3},{7,2},{8,13},{9,12},{10,... | collective-permute-start | bytes 589832 | tf_op jit(solution)/shard_map/ppermute | solution.py:306
  180.3 65.5 %copy-start.1 = (f32[192,256]{1,0:T(8,128)}, f32[192,256]{1,0:T(8,128)S(1)}, u32[]{:S(2)}) copy-start(f32[192,256]{1,0:T(8,128)S(1)} %collective-permute-done.refs_1_) | copy-start | bytes 589828
  180.3 65.6 %collective-permute-start.5 = (f32[192,256]{1,0:T(8,128)S(1)}, f32[192,256]{1,0:T(8,128)S(1)}, u32[]{:S(2)}, u32[]{:S(2)}) collective-permute-start(f32[192,256]{1,0:T(8,128)S(1)} %get-tuple-element.29), channel_id=1, source_target_pairs={{0,6},{1,7},{2,4},{3,5},{4,2},{5,3},{6,0},{7,1},{8,14},{9,15},{10,... | collective-permute-start | bytes 589832 | tf_op jit(solution)/shard_map/ppermute | solution.py:306
  185.9 59.9 %copy-start.2 = (f32[192,256]{1,0:T(8,128)}, f32[192,256]{1,0:T(8,128)S(1)}, u32[]{:S(2)}) copy-start(f32[192,256]{1,0:T(8,128)S(1)} %collective-permute-done.1.refs_2_) | copy-start | bytes 589828
  185.9 60.0 %collective-permute-start.6 = (f32[192,256]{1,0:T(8,128)S(1)}, f32[192,256]{1,0:T(8,128)S(1)}, u32[]{:S(2)}, u32[]{:S(2)}) collective-permute-start(f32[192,256]{1,0:T(8,128)S(1)} %get-tuple-element.28), channel_id=1, source_target_pairs={{0,7},{1,6},{2,5},{3,4},{4,3},{5,2},{6,1},{7,0},{8,15},{9,14},{10,... | collective-permute-start | bytes 589832 | tf_op jit(solution)/shard_map/ppermute | solution.py:306
  245.8 0.7 copy-start.3
  245.9 0.7 copy-start.4
  245.9 0.8 copy-start.5
  245.9 0.8 copy-start.6
  245.9 0.9 copy-start.7
  251.9 266.5 %all-gather.11.cloned.1.call-start = ((), (), s32[]{:S(2)}) async-start(), calls=%async_computation.1 | async-start | bytes 3538944 | tf_op jit(solution)/shard_map/all_gather | solution.py:356
  409.0 193.7 %all-gather.17.cloned.1.call-start = ((), (), s32[]{:S(2)}) async-start(), calls=%async_computation.4 | async-start | bytes 11796480 | tf_op jit(solution)/shard_map/all_gather | solution.py:391
  410.5 90.4 %copy-start = (f32[512,768]{1,0:T(8,128)}, f32[512,768]{1,0:T(8,128)S(1)}, u32[]{:S(2)}) copy-start(f32[512,768]{1,0:T(8,128)S(1)} %slice.15.refs_0_) | copy-start | bytes 4718596
  410.6 73.4 %collective-permute-start.7 = (f32[512,768]{1,0:T(8,128)S(1)}, f32[512,768]{1,0:T(8,128)S(1)}, u32[]{:S(2)}, u32[]{:S(2)}) collective-permute-start(f32[512,768]{1,0:T(8,128)S(1)} %slice.15.refs_0_), channel_id=1, source_target_pairs={{0,8},{1,9},{2,10},{3,11},{4,12},{5,13},{6,14},{7,15},{8,0},{9,1},... | collective-permute-start | bytes 4718600 | tf_op jit(solution)/shard_map/ppermute | solution.py:306
  421.7 62.3 %collective-permute-start.8 = (f32[512,768]{1,0:T(8,128)S(1)}, f32[512,768]{1,0:T(8,128)S(1)}, u32[]{:S(2)}, u32[]{:S(2)}) collective-permute-start(f32[512,768]{1,0:T(8,128)S(1)} %slice.15.refs_0_), channel_id=1, source_target_pairs={{0,16},{1,17},{2,18},{3,19},{4,20},{5,21},{6,22},{7,23},{8,24},{9,... | collective-permute-start | bytes 4718600 | tf_op jit(solution)/shard_map/ppermute | solution.py:306
  421.7 79.2 %collective-permute-start.9 = (f32[512,768]{1,0:T(8,128)S(1)}, f32[512,768]{1,0:T(8,128)S(1)}, u32[]{:S(2)}, u32[]{:S(2)}) collective-permute-start(f32[512,768]{1,0:T(8,128)S(1)} %slice.15.refs_0_), channel_id=1, source_target_pairs={{0,24},{1,25},{2,26},{3,27},{4,28},{5,29},{6,30},{7,31},{8,16},{9,... | collective-permute-start | bytes 4718600 | tf_op jit(solution)/shard_map/ppermute | solution.py:306
  484.0 17.0 %copy-start.12 = (f32[512,768]{1,0:T(8,128)}, f32[512,768]{1,0:T(8,128)S(1)}, u32[]{:S(2)}) copy-start(f32[512,768]{1,0:T(8,128)S(1)} %collective-permute-done.7.refs_1_) | copy-start | bytes 4718596
  484.0 17.0 %copy-start.13 = (f32[512,768]{1,0:T(8,128)}, f32[512,768]{1,0:T(8,128)S(1)}, u32[]{:S(2)}) copy-start(f32[512,768]{1,0:T(8,128)S(1)} %collective-permute-done.8.refs_2_) | copy-start | bytes 4718596
  500.9 1.2 copy-start.14
  531.8 0.7 copy-start.11
  531.8 2.6 copy-start.15
  531.8 3.2 copy-start.8
  531.9 3.2 copy-start.9
  531.9 3.2 copy-start.10
Sparse Core Ops, SparseCore 0:
  10.2 152.1 all-gather.12
  164.2 169.9 all-gather.14
  336.4 52.6 all-gather.8
  409.1 53.0 all-gather.10
  532.0 70.6 all-gather.16
